TPU v7x, 32 devices: a whole 2x2x4 slice. The times are simulated.
32 devices in a mesh: dp: 4 (over x, core), cp: 8 (over z, y).
Axes of the slice: x: 2, y: 2, z: 4, core: 2. Of those that a mesh axis runs over, the one named last changes fastest.
Arguments:
- q_raw: bfloat16 [4096, 4096], P(('dp', 'cp')), may hold values from -60 to 60
- k_raw: bfloat16 [4096, 512], P(('dp', 'cp')), may hold values from -60 to 60
- values: bfloat16 [4096, 512], P(('dp', 'cp')), may hold values from -6 to 6
- loss_grad: bfloat16 [4096, 4096], P(('dp', 'cp')), may hold values from -6 to 6
- send_order: int32 [32, 128], P(('dp', 'cp')), may hold values from 0 to 127, each once within a row
- doc_blocks: int32 [4, 8], P('dp', 'cp'), may hold values from 0 to 2, never falling along the last dimension, each value on 1 to 5 neighbouring positions
- gain_q: float32 [128], replicated, may hold values from 0.6 to 4.6
- gain_k: float32 [128], replicated, may hold values from 0.6 to 4.6
Outputs:
- attn_out: bfloat16 [4096, 4096], P(('dp', 'cp'))
- dq_raw: bfloat16 [4096, 4096], P(('dp', 'cp'))
- dk_raw: bfloat16 [4096, 512], P(('dp', 'cp'))
- dv_out: bfloat16 [4096, 512], P(('dp', 'cp'))
- dgain_q: float32 [128], replicated
- dgain_k: float32 [128], replicated
Inputs may be any that keep to these rules, and one draw needn't show every extreme that they name: `send_order`: each row is a permutation of 0 to 127. `doc_blocks`: within each row ids never fall, every id 0 to 2 occurs, each document covers 1 to 5 consecutive blocks, and some document covers exactly 5.
All inputs are finite; a program needn't handle non-finite values.
Results may differ from a plain program's by a relative error of at most 0.033.
The roundings to bfloat16 on the way count: a program that leaves them out, or rounds other values in their place, can miss the bound.
Values may be sent and summed in bfloat16 or wider, within the bound.
A program may use at most 128 MiB of HBM per device.

v0:
```python
import functools
import math

import jax
import jax.numpy as jnp
import numpy as np
from jax import lax
from jax.experimental import pallas as pl
from jax.experimental.pallas import tpu as pltpu
from jax.sharding import PartitionSpec as P

MOST_BLK = 5
EPSILON = 1e-06
THETA = 1000000.0
NEGATIVE = -1e30
MESH = pl.DeviceIdType.MESH
F32 = jnp.float32
BF16 = jnp.bfloat16


def dot(a, b):
    return jnp.dot(a, b, preferred_element_type=F32)


def dot_nt(a, b):
    return lax.dot_general(a, b, (((1,), (1,)), ((), ())), preferred_element_type=F32)


def flip(x, d):
    parts = [x[:, i : i + d].T for i in range(0, x.shape[1], d)]
    return parts[0] if len(parts) == 1 else jnp.concatenate(parts, axis=1)


def wide(x, n):
    return x if n == 1 else jnp.concatenate([x] * n, axis=1)


def rotate(x, cos, sin):
    half = x.shape[0] // 2
    lead, trail = x[:half], x[half:]
    return jnp.concatenate([lead * cos - trail * sin, trail * cos + lead * sin], axis=0)


def unrotate(x, cos, sin):
    half = x.shape[0] // 2
    lead, trail = x[:half], x[half:]
    return jnp.concatenate([lead * cos + trail * sin, trail * cos - lead * sin], axis=0)


def unit_of(x):
    inv = lax.rsqrt(jnp.mean(x * x, axis=0, keepdims=True) + EPSILON)
    return x * inv, inv


def norm_back(cot, unit, inv, gain):
    scaled = cot * gain
    inner = jnp.mean(scaled * unit, axis=0, keepdims=True)
    return inv * (scaled - unit * inner)


def kernel(
    n_dp, n_cp, kv, grp, d, tok, pair,
    q_hbm, k_hbm, v_hbm, g_hbm, order_ref, doc_ref, gq_ref, gk_ref, table_ref,
    out_hbm, dq_hbm, dk_ref, dv_ref, gains_q_ref, gains_k_ref,
    q_in, k_in, v_in, g_in, hot, kv_send, kv_recv, qg_send, qg_recv,
    id_send, id_recv, ring_send, ring_recv, keys, vals, keys_t, vals_t,
    grad_send, grad_recv, dk_own, dv_own, dk_sum, dv_sum, k_unit, k_inv,
    cos_ref, sin_ref, gq_t, gk_t, tri, out_buf, dq_buf, acc_q, part, tot, dp_recv, cp_recv,
    in_sem, out_sem, kvs_sem, kvr_sem, qgs_sem, qgr_sem, ids_sem, idr_sem,
    rs_sem, rr_sem, gs_sem, gr_sem, ds_sem, dr_sem, cs_sem, cr_sem,
):
    a = lax.axis_index("dp")
    c = lax.axis_index("cp")
    reach = min(MOST_BLK - 1, n_cp - 1)
    blocks = reach + 1
    width = grp * d
    rows = tok // n_dp
    inv_root = 1.0 / math.sqrt(d)
    exp_scale = inv_root * math.log2(math.e)

    def columns(h, size):
        return pl.ds(pl.multiple_of(h * size, size), size)

    def in_copy(h, src, dst, which):
        return pltpu.make_async_copy(
            src.at[:, columns(h, width)], dst.at[:, columns(h, width)], in_sem.at[2 + which, h]
        )

    k_copy = pltpu.make_async_copy(k_hbm, k_in, in_sem.at[0, 0])
    v_copy = pltpu.make_async_copy(v_hbm, v_in, in_sem.at[1, 0])
    k_copy.start()
    v_copy.start()
    for h in range(kv):
        in_copy(h, q_hbm, q_in, 0).start()
        in_copy(h, g_hbm, g_in, 1).start()

    barrier = pltpu.get_barrier_semaphore()
    for r in range(1, n_dp):
        pl.semaphore_signal(
            barrier, inc=1, device_id={"dp": lax.rem(a + r, n_dp)}, device_id_type=MESH
        )

    def greet(r, carry):
        pl.semaphore_signal(
            barrier, inc=1, device_id={"cp": lax.rem(c + r, n_cp)}, device_id_type=MESH
        )
        return carry

    lax.fori_loop(1, n_cp, greet, 0)

    own_id = jnp.broadcast_to(doc_ref[...], (8, 128))
    id_send[...] = own_id
    order = jnp.broadcast_to(order_ref[...], (tok, tok)).astype(F32).T
    slot = lax.broadcasted_iota(jnp.int32, (tok, tok), 1)
    hot[...] = jnp.where(order == slot.astype(F32), 1.0, 0.0).astype(BF16)
    gq_t[...] = jnp.broadcast_to(gq_ref[...], (d, d)).T
    gk_t[...] = jnp.broadcast_to(gk_ref[...], (d, d)).T
    tri[...] = jnp.where(
        lax.broadcasted_iota(jnp.int32, (tok, tok), 0)
        <= lax.broadcasted_iota(jnp.int32, (tok, tok), 1),
        0.0,
        NEGATIVE,
    )
    acc_q[...] = jnp.zeros_like(acc_q)
    for s in range(1, blocks):

        @pl.when(c < s)
        def _():
            id_recv[s - 1] = jnp.zeros((8, 128), jnp.int32)
            for h in range(kv):
                ring_recv[h, s - 1] = jnp.zeros((tok, 2 * d), BF16)

        @pl.when(c + s >= n_cp)
        def _():
            for h in range(kv):
                grad_recv[h, s - 1] = jnp.zeros((tok, 2 * d), BF16)

    k_copy.wait()
    v_copy.wait()
    kw = kv * d
    kv_send[:, :kw] = dot(hot[...], k_in[...]).astype(BF16)
    kv_send[:, kw:] = dot(hot[...], v_in[...]).astype(BF16)
    mine = pl.ds(pl.multiple_of(a * rows, rows), rows)
    kv_recv[mine, :] = kv_send[mine, :]

    pl.semaphore_wait(barrier, n_dp - 1 + n_cp - 1)

    def kv_copy(r):
        peer = lax.rem(a + r, n_dp)
        return pltpu.make_async_remote_copy(
            src_ref=kv_send.at[pl.ds(pl.multiple_of(peer * rows, rows), rows), :],
            dst_ref=kv_recv.at[mine, :],
            send_sem=kvs_sem.at[r - 1],
            recv_sem=kvr_sem.at[r - 1],
            device_id={"dp": peer},
            device_id_type=MESH,
        )

    def qg_copy(h, r):
        peer = lax.rem(a + r, n_dp)
        return pltpu.make_async_remote_copy(
            src_ref=qg_send.at[h, pl.ds(pl.multiple_of(peer * rows, rows), rows), :],
            dst_ref=qg_recv.at[h, mine, :],
            send_sem=qgs_sem.at[h, r - 1],
            recv_sem=qgr_sem.at[h, r - 1],
            device_id={"dp": peer},
            device_id_type=MESH,
        )

    def id_copy(s):
        return pltpu.make_async_remote_copy(
            src_ref=id_send,
            dst_ref=id_recv.at[s - 1],
            send_sem=ids_sem.at[s - 1],
            recv_sem=idr_sem.at[s - 1],
            device_id={"cp": lax.rem(c + s, n_cp)},
            device_id_type=MESH,
        )

    def ring_copy(h, s):
        return pltpu.make_async_remote_copy(
            src_ref=ring_send.at[h],
            dst_ref=ring_recv.at[h, s - 1],
            send_sem=rs_sem.at[h, s - 1],
            recv_sem=rr_sem.at[h, s - 1],
            device_id={"cp": lax.rem(c + s, n_cp)},
            device_id_type=MESH,
        )

    def grad_copy(h, s):
        return pltpu.make_async_remote_copy(
            src_ref=grad_send.at[h, s - 1],
            dst_ref=grad_recv.at[h, s - 1],
            send_sem=gs_sem.at[h, s - 1],
            recv_sem=gr_sem.at[h, s - 1],
            device_id={"cp": lax.rem(c + n_cp - s, n_cp)},
            device_id_type=MESH,
        )

    for r in range(1, n_dp):
        kv_copy(r).start()
    for s in range(1, blocks):

        @pl.when(c + s < n_cp)
        def _():
            id_copy(s).start()

    def gather(h, carry):
        in_copy(h, q_hbm, q_in, 0).wait()
        in_copy(h, g_hbm, g_in, 1).wait()
        qg_send[h, :, :width] = dot(hot[...], q_in[:, columns(h, width)]).astype(BF16)
        qg_send[h, :, width:] = dot(hot[...], g_in[:, columns(h, width)]).astype(BF16)
        qg_recv[h, mine, :] = qg_send[h, mine, :]
        for r in range(1, n_dp):
            qg_copy(h, r).start()
        return carry

    lax.fori_loop(0, kv, gather, 0)

    for s in range(1, blocks):

        @pl.when(c >= s)
        def _():
            id_copy(s).wait_recv()

    before = jnp.zeros((1, 128), F32)
    away = []
    for s in range(1, blocks):
        here = (c >= s).astype(F32)
        same = jnp.where(id_recv[s - 1, 0:1, :] == own_id[0:1, :], here, 0.0)
        before = before + same
        away.append(wide((1.0 - same) * -NEGATIVE, pair))
    half = d // 2
    cos = jnp.zeros((half, tok), F32)
    sin = jnp.zeros((half, tok), F32)
    for s in range(MOST_BLK):
        hit = before == float(s)
        cos = cos + jnp.where(hit, table_ref[:half, s * tok : (s + 1) * tok], 0.0)
        sin = sin + jnp.where(hit, table_ref[half:, s * tok : (s + 1) * tok], 0.0)
    cos_ref[...] = cos
    sin_ref[...] = sin

    for r in range(1, n_dp):
        kv_copy(r).wait_recv()

    for h in range(kv):
        x = kv_recv[:, h * d : (h + 1) * d].astype(F32).T
        unit, inv = unit_of(x)
        k_unit[h] = unit
        k_inv[h] = jnp.broadcast_to(inv, (8, tok))
        turned = rotate(unit * gk_t[...], cos_ref[...], sin_ref[...])
        ring_send[h, :, :d] = turned.T.astype(BF16)
        ring_send[h, :, d:] = kv_recv[:, kw + h * d : kw + (h + 1) * d]
        for s in range(1, blocks):

            @pl.when(c + s < n_cp)
            def _():
                ring_copy(h, s).start()

    def out_copy(h, src, dst, which):
        return pltpu.make_async_copy(
            src.at[:, columns(h, width)], dst.at[:, columns(h, width)], out_sem.at[which, h]
        )

    span = pair * d

    def head(h, carry):
        for r in range(1, n_dp):
            qg_copy(h, r).wait_recv()
        for s in range(1, blocks):

            @pl.when(c >= s)
            def _():
                ring_copy(h, s).wait_recv()

        for s in range(blocks):
            both = ring_send[h] if s == 0 else ring_recv[h, s - 1]
            keys[s * tok : (s + 1) * tok, :] = both[:, :d]
            vals[s * tok : (s + 1) * tok, :] = both[:, d:]
            keys_t[:, s * tok : (s + 1) * tok] = both[:, :d].T
            vals_t[:, s * tok : (s + 1) * tok] = both[:, d:].T
        dk_own[...] = jnp.zeros_like(dk_own)
        dv_own[...] = jnp.zeros_like(dv_own)

        def some(j, carry):
            cos = wide(cos_ref[...], pair)
            sin = wide(sin_ref[...], pair)
            gain = wide(gq_t[...], pair)
            unit, inv = unit_of(flip(qg_recv[h, :, columns(j, span)].astype(F32), d))
            turned = rotate(unit * gain, cos, sin).astype(BF16)
            g_at = pl.ds(pl.multiple_of(width + j * span, span), span)
            g_t = flip(qg_recv[h, :, g_at], d)
            scores = dot(keys[...], turned)
            parts = [scores[s * tok : (s + 1) * tok] for s in range(blocks)]
            parts[0] = parts[0] + wide(tri[...], pair)
            top = jnp.max(parts[0], axis=0, keepdims=True)
            for s in range(1, blocks):
                top = jnp.maximum(top, jnp.max(parts[s], axis=0, keepdims=True) - away[s - 1])
            weights = [
                jnp.exp2((parts[s] - (top if s == 0 else top + away[s - 1])) * exp_scale)
                for s in range(blocks)
            ]
            weights = jnp.concatenate(weights, axis=0)
            inv_sum = 1.0 / jnp.sum(weights, axis=0, keepdims=True)
            out_t = (dot(vals_t[...], weights.astype(BF16)) * inv_sum).astype(BF16)
            delta = jnp.sum(g_t.astype(F32) * out_t.astype(F32), axis=0, keepdims=True)
            probs = weights * inv_sum
            dprobs = dot(vals[...], g_t)
            dscores = (probs * (dprobs - delta)).astype(BF16)
            dk_own[...] += dot_nt(dscores, turned)
            dv_own[...] += dot_nt(probs.astype(BF16), g_t)
            dqn = unrotate(dot(keys_t[...], dscores) * inv_root, cos, sin)
            term = dqn * unit
            acc_q[...] += sum(term[:, i * d : (i + 1) * d] for i in range(pair))
            at = pl.ds(pl.multiple_of(h * width + j * span, span), span)
            out_buf[:, at] = flip(out_t, d)
            dq_buf[:, at] = flip(norm_back(dqn, unit, inv, gain).astype(BF16), d)
            return carry

        lax.fori_loop(0, grp // pair, some, 0)
        for s in range(1, blocks):
            at = slice(s * tok, (s + 1) * tok)
            grad_send[h, s - 1, :, :d] = (dk_own[at, :] * inv_root).astype(BF16)
            grad_send[h, s - 1, :, d:] = dv_own[at, :].astype(BF16)

            @pl.when(c >= s)
            def _():
                grad_copy(h, s).start()

        dk_sum[h] = dk_own[:tok, :] * inv_root
        dv_sum[h] = dv_own[:tok, :]
        out_copy(h, out_buf, out_hbm, 0).start()
        out_copy(h, dq_buf, dq_hbm, 1).start()
        return carry

    lax.fori_loop(0, kv, head, 0)

    acc_k = jnp.zeros((d, tok), F32)
    for h in range(kv):
        for s in range(1, blocks):

            @pl.when(c + s < n_cp)
            def _():
                grad_copy(h, s).wait_recv()

        dk = dk_sum[h]
        dv = dv_sum[h]
        for s in range(1, blocks):
            dk = dk + grad_recv[h, s - 1, :, :d].astype(F32)
            dv = dv + grad_recv[h, s - 1, :, d:].astype(F32)
        at = slice(h * d, (h + 1) * d)
        dv_ref[:, at] = dv.astype(BF16)
        dkn = unrotate(dk.T, cos_ref[...], sin_ref[...])
        acc_k = acc_k + dkn * k_unit[h]
        dk_ref[:, at] = norm_back(dkn, k_unit[h], k_inv[h, 0:1, :], gk_t[...]).T.astype(BF16)

    part[...] = jnp.concatenate(
        [
            jnp.sum(acc_q[...].T, axis=0, keepdims=True),
            jnp.sum(acc_k.T, axis=0, keepdims=True),
            jnp.zeros((6, d), F32),
        ],
        axis=0,
    )
    dp_recv[a] = part[...]

    def dp_copy(r):
        return pltpu.make_async_remote_copy(
            src_ref=part,
            dst_ref=dp_recv.at[a],
            send_sem=ds_sem.at[r - 1],
            recv_sem=dr_sem.at[r - 1],
            device_id={"dp": lax.rem(a + r, n_dp)},
            device_id_type=MESH,
        )

    def cp_copy(r):
        return pltpu.make_async_remote_copy(
            src_ref=tot,
            dst_ref=cp_recv.at[c],
            send_sem=cs_sem.at[r - 1],
            recv_sem=cr_sem.at[r - 1],
            device_id={"cp": lax.rem(c + r, n_cp)},
            device_id_type=MESH,
        )

    for r in range(1, n_dp):
        dp_copy(r).start()
    for r in range(1, n_dp):
        dp_copy(r).wait_recv()
    total = dp_recv[0]
    for r in range(1, n_dp):
        total = total + dp_recv[r]
    tot[...] = total
    cp_recv[c] = total

    def each(act):
        def step(r, carry):
            act(cp_copy(r))
            return carry

        lax.fori_loop(1, n_cp, step, 0)

    each(lambda copy: copy.start())

    for r in range(1, n_dp):
        kv_copy(r).wait_send()
        dp_copy(r).wait_send()
    for s in range(1, blocks):

        @pl.when(c + s < n_cp)
        def _():
            id_copy(s).wait_send()

    def settle(h, carry):
        for r in range(1, n_dp):
            qg_copy(h, r).wait_send()
        for s in range(1, blocks):

            @pl.when(c + s < n_cp)
            def _():
                ring_copy(h, s).wait_send()

            @pl.when(c >= s)
            def _():
                grad_copy(h, s).wait_send()

        out_copy(h, out_buf, out_hbm, 0).wait()
        out_copy(h, dq_buf, dq_hbm, 1).wait()
        return carry

    lax.fori_loop(0, kv, settle, 0)
    each(lambda copy: copy.wait())
    total = lax.fori_loop(1, n_cp, lambda r, sofar: sofar + cp_recv[r], cp_recv[0])
    total = total * (1.0 / math.sqrt(tok * n_dp * n_cp))
    gains_q_ref[...] = total[0:1, :]
    gains_k_ref[...] = total[1:2, :]


def body(n_dp, n_cp, q_raw, k_raw, values, loss_grad, send_order, doc_blocks, gain_q, gain_k):
    tok, q_width = q_raw.shape
    kw = k_raw.shape[1]
    d = gain_q.shape[0]
    kv = kw // d
    grp = q_width // kw
    blocks = min(MOST_BLK, n_cp)
    reach = blocks - 1
    pair = 2 if grp % 2 == 0 else 1
    assert doc_blocks.shape == (1, 1)
    frequency = THETA ** (-(np.arange(d // 2, dtype=np.float64) * 2.0 / d))
    angles = frequency[:, None] * np.arange(MOST_BLK * tok, dtype=np.float64)[None, :]
    table = jnp.asarray(np.concatenate([np.cos(angles), np.sin(angles)]).astype(np.float32))
    vmem = pl.BlockSpec(memory_space=pltpu.VMEM)
    hbm = pl.BlockSpec(memory_space=pl.ANY)
    dma = pltpu.SemaphoreType.DMA
    V = pltpu.VMEM
    outs = pl.pallas_call(
        functools.partial(kernel, n_dp, n_cp, kv, grp, d, tok, pair),
        out_shape=[
            jax.ShapeDtypeStruct((tok, q_width), BF16),
            jax.ShapeDtypeStruct((tok, q_width), BF16),
            jax.ShapeDtypeStruct((tok, kw), BF16),
            jax.ShapeDtypeStruct((tok, kw), BF16),
            jax.ShapeDtypeStruct((1, d), F32),
            jax.ShapeDtypeStruct((1, d), F32),
        ],
        in_specs=[hbm] * 4 + [vmem] * 5,
        out_specs=[hbm] * 2 + [vmem] * 4,
        scratch_shapes=[
            V((tok, q_width), BF16),
            V((tok, kw), BF16),
            V((tok, kw), BF16),
            V((tok, q_width), BF16),
            V((tok, tok), BF16),
            V((tok, 2 * kw), BF16),
            V((tok, 2 * kw), BF16),
            V((kv, tok, 2 * grp * d), BF16),
            V((kv, tok, 2 * grp * d), BF16),
            V((8, 128), jnp.int32),
            V((reach, 8, 128), jnp.int32),
            V((kv, tok, 2 * d), BF16),
            V((kv, reach, tok, 2 * d), BF16),
            V((blocks * tok, d), BF16),
            V((blocks * tok, d), BF16),
            V((d, blocks * tok), BF16),
            V((d, blocks * tok), BF16),
            V((kv, reach, tok, 2 * d), BF16),
            V((kv, reach, tok, 2 * d), BF16),
            V((blocks * tok, d), F32),
            V((blocks * tok, d), F32),
            V((kv, tok, d), F32),
            V((kv, tok, d), F32),
            V((kv, d, tok), F32),
            V((kv, 8, tok), F32),
            V((d // 2, tok), F32),
            V((d // 2, tok), F32),
            V((d, d), F32),
            V((d, d), F32),
            V((tok, tok), F32),
            V((tok, q_width), BF16),
            V((tok, q_width), BF16),
            V((d, tok), F32),
            V((8, d), F32),
            V((8, d), F32),
            V((n_dp, 8, d), F32),
            V((n_cp, 8, d), F32),
            dma((4, kv)),
            dma((2, kv)),
            dma((n_dp - 1,)),
            dma((n_dp - 1,)),
            dma((kv, n_dp - 1)),
            dma((kv, n_dp - 1)),
            dma((reach,)),
            dma((reach,)),
            dma((kv, reach)),
            dma((kv, reach)),
            dma((kv, reach)),
            dma((kv, reach)),
            dma((n_dp - 1,)),
            dma((n_dp - 1,)),
            dma((n_cp - 1,)),
            dma((n_cp - 1,)),
        ],
        compiler_params=pltpu.CompilerParams(
            collective_id=0, has_side_effects=True, vmem_limit_bytes=44 * 1024 * 1024
        ),
    )(
        q_raw, k_raw, values, loss_grad, send_order, doc_blocks,
        gain_q.reshape(1, d), gain_k.reshape(1, d), table,
    )
    return (*outs[:4], outs[4].reshape(d), outs[5].reshape(d))


def solution(mesh):
    split = P(("dp", "cp"), None)
    return jax.shard_map(
        functools.partial(body, mesh.shape["dp"], mesh.shape["cp"]),
        mesh=mesh,
        in_specs=(split,) * 5 + (P("dp", "cp"), P(), P()),
        out_specs=(split,) * 4 + (P(), P()),
        check_vma=False,
    )
```

profile of v0, /device:TPU:0, one launch (start us, length us, event | category | flops | bytes accessed | tf_op | source)
XLA Modules:
  0.0 80.3 jit_solution(3519106563986568960)
XLA Ops:
  1.3 0.0 copy-start.5
  1.3 0.0 copy-start.6
  1.3 0.0 copy-start.7
  1.3 0.6 copy-done.5
  1.9 0.0 copy-done.6
  2.0 0.0 copy-done.7
  2.0 0.0 copy-start
  2.0 1.2 %copy-done = bf16[128,4096]{1,0:T(8,128)(2,1)S(1)} copy-done((bf16[128,4096]{1,0:T(8,128)(2,1)S(1)}, bf16[128,4096]{1,0:T(8,128)(2,1)}, u32[]{:S(2)}) %copy-start) | copy-done | bytes 1048600
  3.2 0.0 copy-start.1
  3.2 1.2 %copy-done.1 = bf16[128,4096]{1,0:T(8,128)(2,1)S(1)} copy-done((bf16[128,4096]{1,0:T(8,128)(2,1)S(1)}, bf16[128,4096]{1,0:T(8,128)(2,1)}, u32[]{:S(2)}) %copy-start.1) | copy-done | bytes 1048600
  4.4 0.0 copy-start.2
  4.4 1.0 %copy-done.2 = f32[128,640]{1,0:T(8,128)S(1)} copy-done((f32[128,640]{1,0:T(8,128)S(1)}, f32[128,640]{1,0:T(8,128)}, u32[]{:S(2)}) %copy-start.2) | copy-done | bytes 327704
  5.4 0.0 copy-start.3
  5.4 0.9 %copy-done.3 = bf16[128,512]{1,0:T(8,128)(2,1)S(1)} copy-done((bf16[128,512]{1,0:T(8,128)(2,1)S(1)}, bf16[128,512]{1,0:T(8,128)(2,1)}, u32[]{:S(2)}) %copy-start.3) | copy-done | bytes 131096
  6.3 0.0 copy-start.4
  6.3 0.9 %copy-done.4 = bf16[128,512]{1,0:T(8,128)(2,1)S(1)} copy-done((bf16[128,512]{1,0:T(8,128)(2,1)S(1)}, bf16[128,512]{1,0:T(8,128)(2,1)}, u32[]{:S(2)}) %copy-start.4) | copy-done | bytes 131096
  7.2 68.8 %shard_map.136 = (bf16[128,4096]{1,0:T(8,128)(2,1)S(1)}, bf16[128,4096]{1,0:T(8,128)(2,1)S(1)}, bf16[128,512]{1,0:T(8,128)(2,1)S(1)}, bf16[128,512]{1,0:T(8,128)...) custom-call(bf16[128,4096]{1,0:T(8,128)(2,1)S(1)} %copy-done, bf16[128,512]{1,0:T(8,128)(2,1)S(1)} %copy-done.3, ...), custom_call_target="tpu_custom_call" | custom-call | tf_op jit(solution)/shard_map/pallas_call | solution.py:457
  76.1 1.0 %copy.22 = bf16[128,4096]{1,0:T(8,128)(2,1)} copy(bf16[128,4096]{1,0:T(8,128)(2,1)S(1)} %get-tuple-element.24) | data formatting | bytes 2097152
  77.0 1.0 %copy.23 = bf16[128,4096]{1,0:T(8,128)(2,1)} copy(bf16[128,4096]{1,0:T(8,128)(2,1)S(1)} %get-tuple-element.25) | data formatting | bytes 2097152
  78.0 0.7 copy.24
  78.7 0.7 copy.25
  79.3 0.5 copy.26
  79.8 0.5 copy.27
Async XLA Ops:
  1.3 0.7 copy-start.5
  1.3 0.7 copy-start.6
  1.3 0.7 copy-start.7
  2.0 1.2 %copy-start = (bf16[128,4096]{1,0:T(8,128)(2,1)S(1)}, bf16[128,4096]{1,0:T(8,128)(2,1)}, u32[]{:S(2)}) copy-start(bf16[128,4096]{1,0:T(8,128)(2,1)} %q_hbm.1) | copy-start | bytes 3145732
  3.2 1.2 %copy-start.1 = (bf16[128,4096]{1,0:T(8,128)(2,1)S(1)}, bf16[128,4096]{1,0:T(8,128)(2,1)}, u32[]{:S(2)}) copy-start(bf16[128,4096]{1,0:T(8,128)(2,1)} %g_hbm.1) | copy-start | bytes 3145732
  4.4 1.0 %copy-start.2 = (f32[128,640]{1,0:T(8,128)S(1)}, f32[128,640]{1,0:T(8,128)}, u32[]{:S(2)}) copy-start(f32[128,640]{1,0:T(8,128)} %constant.2.clone.table_ref) | copy-start | bytes 983044
  5.4 0.9 %copy-start.3 = (bf16[128,512]{1,0:T(8,128)(2,1)S(1)}, bf16[128,512]{1,0:T(8,128)(2,1)}, u32[]{:S(2)}) copy-start(bf16[128,512]{1,0:T(8,128)(2,1)} %k_hbm.1) | copy-start | bytes 393220
  6.3 0.9 %copy-start.4 = (bf16[128,512]{1,0:T(8,128)(2,1)S(1)}, bf16[128,512]{1,0:T(8,128)(2,1)}, u32[]{:S(2)}) copy-start(bf16[128,512]{1,0:T(8,128)(2,1)} %v_hbm.1) | copy-start | bytes 393220
where the time goes:
time: 80.6 us; the launch traced here: 80.3 us
  Pallas kernels  68.8 us (85%)
  local copies, waits for them, and re-layouts  10.2 us (13%)
  between operations  1.32 us (2%)
    pallas_call x1, Pallas kernels, body(): pl.pallas_call(functools.partial(kernel, n_dp, n_cp, kv, grp, d, tok, pai...  68.8 us
    unnamed x22, local copies, waits for them, and re-layouts  10.2 us

commit v1 on v0

--- a/solution.py
+++ b/solution.py
@@ -60,19 +60,20 @@
 
 def kernel(
     n_dp, n_cp, kv, grp, d, tok, pair,
-    q_hbm, k_hbm, v_hbm, g_hbm, order_ref, doc_ref, gq_ref, gk_ref, table_ref,
-    out_hbm, dq_hbm, dk_ref, dv_ref, gains_q_ref, gains_k_ref,
-    q_in, k_in, v_in, g_in, hot, kv_send, kv_recv, qg_send, qg_recv,
+    q_hbm, k_hbm, v_hbm, g_hbm, order_hbm, doc_ref, gq_hbm, gk_hbm, table_hbm,
+    out_hbm, dq_hbm, dk_ref, dv_ref, gains_ref,
+    q_in, k_in, v_in, g_in, order_ref, gq_ref, gk_ref, table_ref, hot, kv_send, kv_recv, qg_send, qg_recv,
     id_send, id_recv, ring_send, ring_recv, keys, vals, keys_t, vals_t,
     grad_send, grad_recv, dk_own, dv_own, dk_sum, dv_sum, k_unit, k_inv,
     cos_ref, sin_ref, gq_t, gk_t, tri, out_buf, dq_buf, acc_q, part, tot, dp_recv, cp_recv,
-    in_sem, out_sem, kvs_sem, kvr_sem, qgs_sem, qgr_sem, ids_sem, idr_sem,
+    small_sem, in_sem, out_sem, kvs_sem, kvr_sem, qgs_sem, qgr_sem, ids_sem, idr_sem,
     rs_sem, rr_sem, gs_sem, gr_sem, ds_sem, dr_sem, cs_sem, cr_sem,
 ):
     a = lax.axis_index("dp")
     c = lax.axis_index("cp")
     reach = min(MOST_BLK - 1, n_cp - 1)
     blocks = reach + 1
+    ahead = 2
     width = grp * d
     rows = tok // n_dp
     inv_root = 1.0 / math.sqrt(d)
@@ -88,8 +89,17 @@
 
     k_copy = pltpu.make_async_copy(k_hbm, k_in, in_sem.at[0, 0])
     v_copy = pltpu.make_async_copy(v_hbm, v_in, in_sem.at[1, 0])
+    small = [
+        pltpu.make_async_copy(src, dst, small_sem.at[i])
+        for i, (src, dst) in enumerate(
+            [(order_hbm, order_ref), (gq_hbm, gq_ref), (gk_hbm, gk_ref), (table_hbm, table_ref)]
+        )
+    ]
+    small[0].start()
     k_copy.start()
     v_copy.start()
+    for copy in small[1:]:
+        copy.start()
     for h in range(kv):
         in_copy(h, q_hbm, q_in, 0).start()
         in_copy(h, g_hbm, g_in, 1).start()
@@ -110,9 +120,12 @@
 
     own_id = jnp.broadcast_to(doc_ref[...], (8, 128))
     id_send[...] = own_id
+    small[0].wait()
     order = jnp.broadcast_to(order_ref[...], (tok, tok)).astype(F32).T
     slot = lax.broadcasted_iota(jnp.int32, (tok, tok), 1)
     hot[...] = jnp.where(order == slot.astype(F32), 1.0, 0.0).astype(BF16)
+    small[1].wait()
+    small[2].wait()
     gq_t[...] = jnp.broadcast_to(gq_ref[...], (d, d)).T
     gk_t[...] = jnp.broadcast_to(gk_ref[...], (d, d)).T
     tri[...] = jnp.where(
@@ -211,8 +224,12 @@
         qg_send[h, :, :width] = dot(hot[...], q_in[:, columns(h, width)]).astype(BF16)
         qg_send[h, :, width:] = dot(hot[...], g_in[:, columns(h, width)]).astype(BF16)
         qg_recv[h, mine, :] = qg_send[h, mine, :]
-        for r in range(1, n_dp):
-            qg_copy(h, r).start()
+
+        @pl.when(h < ahead)
+        def _():
+            for r in range(1, n_dp):
+                qg_copy(h, r).start()
+
         return carry
 
     lax.fori_loop(0, kv, gather, 0)
@@ -230,6 +247,7 @@
         same = jnp.where(id_recv[s - 1, 0:1, :] == own_id[0:1, :], here, 0.0)
         before = before + same
         away.append(wide((1.0 - same) * -NEGATIVE, pair))
+    small[3].wait()
     half = d // 2
     cos = jnp.zeros((half, tok), F32)
     sin = jnp.zeros((half, tok), F32)
@@ -253,7 +271,7 @@
         ring_send[h, :, d:] = kv_recv[:, kw + h * d : kw + (h + 1) * d]
         for s in range(1, blocks):
 
-            @pl.when(c + s < n_cp)
+            @pl.when((c + s < n_cp) & (h < ahead))
             def _():
                 ring_copy(h, s).start()
 
@@ -272,6 +290,16 @@
             @pl.when(c >= s)
             def _():
                 ring_copy(h, s).wait_recv()
+
+        @pl.when(h + ahead < kv)
+        def _():
+            for r in range(1, n_dp):
+                qg_copy(h + ahead, r).start()
+        for s in range(1, blocks):
+
+            @pl.when((c + s < n_cp) & (h + ahead < kv))
+            def _():
+                ring_copy(h + ahead, s).start()
 
         for s in range(blocks):
             both = ring_send[h] if s == 0 else ring_recv[h, s - 1]
@@ -286,10 +314,14 @@
             cos = wide(cos_ref[...], pair)
             sin = wide(sin_ref[...], pair)
             gain = wide(gq_t[...], pair)
-            unit, inv = unit_of(flip(qg_recv[h, :, columns(j, span)].astype(F32), d))
+            unit, inv = unit_of(flip(qg_recv[h, :, columns(j, span)], d).astype(F32))
             turned = rotate(unit * gain, cos, sin).astype(BF16)
             g_at = pl.ds(pl.multiple_of(width + j * span, span), span)
-            g_t = flip(qg_recv[h, :, g_at], d)
+            g_rows = qg_recv[h, :, g_at]
+            g_t = flip(g_rows, d)
+            g_rows = jnp.concatenate(
+                [g_rows[:, i * d : (i + 1) * d] for i in range(pair)], axis=0
+            )
             scores = dot(keys[...], turned)
             parts = [scores[s * tok : (s + 1) * tok] for s in range(blocks)]
             parts[0] = parts[0] + wide(tri[...], pair)
@@ -308,7 +340,7 @@
             dprobs = dot(vals[...], g_t)
             dscores = (probs * (dprobs - delta)).astype(BF16)
             dk_own[...] += dot_nt(dscores, turned)
-            dv_own[...] += dot_nt(probs.astype(BF16), g_t)
+            dv_own[...] += dot(probs.astype(BF16), g_rows)
             dqn = unrotate(dot(keys_t[...], dscores) * inv_root, cos, sin)
             term = dqn * unit
             acc_q[...] += sum(term[:, i * d : (i + 1) * d] for i in range(pair))
@@ -433,8 +465,19 @@
     each(lambda copy: copy.wait())
     total = lax.fori_loop(1, n_cp, lambda r, sofar: sofar + cp_recv[r], cp_recv[0])
     total = total * (1.0 / math.sqrt(tok * n_dp * n_cp))
-    gains_q_ref[...] = total[0:1, :]
-    gains_k_ref[...] = total[1:2, :]
+    gains_ref[...] = total
+
+
+def hand_out(out, dq, dk, dv, gains, out_o, dq_o, dk_o, dv_o, gq_o, gk_o, sem):
+    pairs = [
+        (out, out_o), (dq, dq_o), (dk, dk_o), (dv, dv_o),
+        (gains.at[0:1], gq_o), (gains.at[1:2], gk_o),
+    ]
+    copies = [pltpu.make_async_copy(src, dst, sem.at[i]) for i, (src, dst) in enumerate(pairs)]
+    for copy in copies:
+        copy.start()
+    for copy in copies:
+        copy.wait()
 
 
 def body(n_dp, n_cp, q_raw, k_raw, values, loss_grad, send_order, doc_blocks, gain_q, gain_k):
@@ -445,13 +488,14 @@
     grp = q_width // kw
     blocks = min(MOST_BLK, n_cp)
     reach = blocks - 1
-    pair = 2 if grp % 2 == 0 else 1
+    pair = 4 if grp % 4 == 0 else 1
     assert doc_blocks.shape == (1, 1)
     frequency = THETA ** (-(np.arange(d // 2, dtype=np.float64) * 2.0 / d))
     angles = frequency[:, None] * np.arange(MOST_BLK * tok, dtype=np.float64)[None, :]
     table = jnp.asarray(np.concatenate([np.cos(angles), np.sin(angles)]).astype(np.float32))
     vmem = pl.BlockSpec(memory_space=pltpu.VMEM)
-    hbm = pl.BlockSpec(memory_space=pl.ANY)
+    hbm = pl.BlockSpec(memory_space=pltpu.HBM)
+    anywhere = pl.BlockSpec(memory_space=pl.ANY)
     dma = pltpu.SemaphoreType.DMA
     V = pltpu.VMEM
     outs = pl.pallas_call(
@@ -461,16 +505,19 @@
             jax.ShapeDtypeStruct((tok, q_width), BF16),
             jax.ShapeDtypeStruct((tok, kw), BF16),
             jax.ShapeDtypeStruct((tok, kw), BF16),
-            jax.ShapeDtypeStruct((1, d), F32),
-            jax.ShapeDtypeStruct((1, d), F32),
+            jax.ShapeDtypeStruct((8, d), F32),
         ],
-        in_specs=[hbm] * 4 + [vmem] * 5,
-        out_specs=[hbm] * 2 + [vmem] * 4,
+        in_specs=[hbm] * 5 + [vmem] + [hbm] * 3,
+        out_specs=[anywhere] * 2 + [vmem] * 3,
         scratch_shapes=[
             V((tok, q_width), BF16),
             V((tok, kw), BF16),
             V((tok, kw), BF16),
             V((tok, q_width), BF16),
+            V((1, tok), jnp.int32),
+            V((1, d), F32),
+            V((1, d), F32),
+            V(table.shape, F32),
             V((tok, tok), BF16),
             V((tok, 2 * kw), BF16),
             V((tok, 2 * kw), BF16),
@@ -504,6 +551,7 @@
             V((8, d), F32),
             V((n_dp, 8, d), F32),
             V((n_cp, 8, d), F32),
+            dma((4,)),
             dma((4, kv)),
             dma((2, kv)),
             dma((n_dp - 1,)),
@@ -522,12 +570,21 @@
             dma((n_cp - 1,)),
         ],
         compiler_params=pltpu.CompilerParams(
-            collective_id=0, has_side_effects=True, vmem_limit_bytes=44 * 1024 * 1024
+            collective_id=0, has_side_effects=True, vmem_limit_bytes=60 * 1024 * 1024
         ),
     )(
         q_raw, k_raw, values, loss_grad, send_order, doc_blocks,
         gain_q.reshape(1, d), gain_k.reshape(1, d), table,
     )
+    outs = pl.pallas_call(
+        hand_out,
+        out_shape=[jax.ShapeDtypeStruct(x.shape, x.dtype) for x in outs[:4]]
+        + [jax.ShapeDtypeStruct((1, d), F32)] * 2,
+        in_specs=[anywhere] * 4 + [vmem],
+        out_specs=[hbm] * 6,
+        scratch_shapes=[dma((6,))],
+        compiler_params=pltpu.CompilerParams(vmem_limit_bytes=60 * 1024 * 1024),
+    )(*outs)
     return (*outs[:4], outs[4].reshape(d), outs[5].reshape(d))
 
 

time: 80.6 us -> 142 us (1.76)
  Pallas kernels: 68.8 us -> 141 us
  local copies, waits for them, and re-layouts: 10.2 us -> 0 us
    pallas_call x0 -> x1, Pallas kernels: none -> 73.3 us  [body(): pl.pallas_call(hand_out, out_shape=[jax.ShapeDtypeStruct(x.shape, x.dtype...]
    unnamed x22 -> x0, local copies, waits for them, and re-layouts: 10.2 us -> none
where the time goes in v1:
time: 142 us
  Pallas kernels  141 us (99%)
    pallas_call x1, Pallas kernels, body(): pl.pallas_call(hand_out, out_shape=[jax.ShapeDtypeStruct(x.shape, x.dtype...  73.3 us
    pallas_call x1, Pallas kernels, body(): pl.pallas_call(functools.partial(kernel, n_dp, n_cp, kv, grp, d, tok, pai...  67.5 us

profile of v1, /device:TPU:0, one launch (start us, length us, event | category | flops | bytes accessed | tf_op | source)
XLA Modules:
  0.0 142.1 jit_solution(14114650317989822425)
XLA Ops:
  1.3 67.5 %shard_map.136 = (bf16[128,4096]{1,0:T(8,128)(2,1)}, bf16[128,4096]{1,0:T(8,128)(2,1)}, bf16[128,512]{1,0:T(8,128)(2,1)}, bf16[128,512]{1,0:T(8,128)(2,1)}, f32[8,128]{1,0:T(8,128)}) custom-call(bf16[128,4096]{1,0:T(8,128)(2,1)} %q_hbm.1, bf16[128,512]{1,0:T(8,128)(2,1)} %k_hbm.1, bf16[128,512]{1,0:T(8,128)(2,1)} %v_hbm.1, bf16[128,4096]{1,0:T(8,128)(2,1)} %g_hbm.1, ...), custom_call_target="tpu_custom_call" | custom-call | tf_op jit(solution)/shard_map/pallas_call | solution.py:501
  68.8 73.3 %shard_map.137 = (bf16[128,4096]{1,0:T(8,128)(2,1)}, bf16[128,4096]{1,0:T(8,128)(2,1)}, bf16[128,512]{1,0:T(8,128)(2,1)}, bf16[128,512]{1,0:T(8,128)(2,1)}, f32[1,128]{1,0:T(1,128)}, /*index=5*/f32[1,128]{1,0:T(1,128)}) custom-call(bf16[128,4096]{1,0:T(8,128)(2,1)} %get-tuple-element.17.out, bf16[128,4096]{1,0:T(8,128)(2,1)} %get-tuple-element.18.dq, ...), custom_call_target="tpu_custom_call" | custom-call | tf_op jit(solution)/shard_map/pallas_call | solution.py:579

commit v2 on v1

--- a/solution.py
+++ b/solution.py
@@ -64,20 +64,22 @@
     out_hbm, dq_hbm, dk_ref, dv_ref, gains_ref,
     q_in, k_in, v_in, g_in, order_ref, gq_ref, gk_ref, table_ref, hot, kv_send, kv_recv, qg_send, qg_recv,
     id_send, id_recv, ring_send, ring_recv, keys, vals, keys_t, vals_t,
-    grad_send, grad_recv, dk_own, dv_own, dk_sum, dv_sum, k_unit, k_inv,
+    grad_send, gy_recv, gz_recv, dk_own, dv_own, sums, k_unit, k_inv,
     cos_ref, sin_ref, gq_t, gk_t, tri, out_buf, dq_buf, acc_q, part, tot, dp_recv, cp_recv,
     small_sem, in_sem, out_sem, kvs_sem, kvr_sem, qgs_sem, qgr_sem, ids_sem, idr_sem,
-    rs_sem, rr_sem, gs_sem, gr_sem, ds_sem, dr_sem, cs_sem, cr_sem,
+    rs_sem, rr_sem, gys_sem, gyr_sem, gzs_sem, gzr_sem, ds_sem, dr_sem, cs_sem, cr_sem,
 ):
     a = lax.axis_index("dp")
     c = lax.axis_index("cp")
     reach = min(MOST_BLK - 1, n_cp - 1)
     blocks = reach + 1
-    ahead = 2
+    ahead = min(3, kv)
+    even = lax.rem(c, 2) == 0
+    even_f = even.astype(F32)
+    mate = c + 1 - 2 * lax.rem(c, 2)
     width = grp * d
     rows = tok // n_dp
     inv_root = 1.0 / math.sqrt(d)
-    exp_scale = inv_root * math.log2(math.e)
 
     def columns(h, size):
         return pl.ds(pl.multiple_of(h * size, size), size)
@@ -143,10 +145,18 @@
             for h in range(kv):
                 ring_recv[h, s - 1] = jnp.zeros((tok, 2 * d), BF16)
 
-        @pl.when(c + s >= n_cp)
+    blank = jnp.zeros((tok, 2 * d), BF16)
+    for slot_of, missing in (
+        ((0, 0), mate < 1),
+        ((0, 1), mate < 3),
+        ((1, 0), (c + 2 >= n_cp) | (c < 2)),
+        ((1, 1), c + 2 >= n_cp),
+    ):
+
+        @pl.when(missing)
         def _():
             for h in range(kv):
-                grad_recv[h, s - 1] = jnp.zeros((tok, 2 * d), BF16)
+                (gy_recv if slot_of[0] == 0 else gz_recv)[h, slot_of[1]] = blank
 
     k_copy.wait()
     v_copy.wait()
@@ -190,25 +200,89 @@
             device_id_type=MESH,
         )
 
-    def ring_copy(h, s):
+    def ring_copy(h, src, to, s, kind):
         return pltpu.make_async_remote_copy(
-            src_ref=ring_send.at[h],
+            src_ref=src,
             dst_ref=ring_recv.at[h, s - 1],
-            send_sem=rs_sem.at[h, s - 1],
+            send_sem=rs_sem.at[h, kind],
             recv_sem=rr_sem.at[h, s - 1],
-            device_id={"cp": lax.rem(c + s, n_cp)},
+            device_id={"cp": to},
             device_id_type=MESH,
         )
 
-    def grad_copy(h, s):
+    behind = lax.rem(c + 2, n_cp)
+    front = lax.rem(c + n_cp - 2, n_cp)
+
+    def ring_plan(h):
+        own, two, four = ring_send.at[h], ring_recv.at[h, 1], ring_recv.at[h, 3]
+        return (
+            (ring_copy(h, own, behind, 2, 0), c + 2 < n_cp),
+            (ring_copy(h, own, mate, 1, 2), even),
+            (ring_copy(h, two, behind, 4, 1), (c >= 2) & (c + 2 < n_cp)),
+            (ring_copy(h, two, mate, 3, 3), even & (c >= 2)),
+            (ring_copy(h, two, mate, 1, 2), jnp.logical_not(even) & (c >= 2)),
+            (ring_copy(h, four, mate, 3, 3), jnp.logical_not(even) & (c >= 4)),
+        )
+
+    def ring_arrived(h, s):
+        @pl.when(c >= s)
+        def _():
+            ring_copy(h, ring_send.at[h], mate, s, 0).wait_recv()
+
+    def start_if(plan):
+        copy, wanted = plan
+
+        @pl.when(wanted)
+        def _():
+            copy.start()
+
+    def mate_copy(h, i):
         return pltpu.make_async_remote_copy(
-            src_ref=grad_send.at[h, s - 1],
-            dst_ref=grad_recv.at[h, s - 1],
-            send_sem=gs_sem.at[h, s - 1],
-            recv_sem=gr_sem.at[h, s - 1],
-            device_id={"cp": lax.rem(c + n_cp - s, n_cp)},
+            src_ref=grad_send.at[h, 2 * i],
+            dst_ref=gy_recv.at[h, i],
+            send_sem=gys_sem.at[h, i],
+            recv_sem=gyr_sem.at[h, i],
+            device_id={"cp": mate},
             device_id_type=MESH,
         )
+
+    def front_copy(h, i):
+        return pltpu.make_async_remote_copy(
+            src_ref=grad_send.at[h, 3 - 2 * i],
+            dst_ref=gz_recv.at[h, i],
+            send_sem=gzs_sem.at[h, i],
+            recv_sem=gzr_sem.at[h, i],
+            device_id={"cp": front},
+            device_id_type=MESH,
+        )
+
+    def after_mate(h):
+        for i in range(2):
+
+            @pl.when(mate >= 1 + 2 * i)
+            def _():
+                mate_copy(h, i).wait_recv()
+
+        one = gy_recv[h, 0].astype(F32)
+        three = gy_recv[h, 1].astype(F32)
+        sums[h, 0] = sums[h, 0] + one * even_f
+        sums[h, 1] = sums[h, 1] + three * even_f + one * (1.0 - even_f)
+        grad_send[h, 3] = (sums[h, 2] + three * (1.0 - even_f)).astype(BF16)
+
+        @pl.when(c >= 4)
+        def _():
+            front_copy(h, 0).start()
+
+    def after_four(h):
+        @pl.when((c + 2 < n_cp) & (c >= 2))
+        def _():
+            front_copy(h, 0).wait_recv()
+
+        grad_send[h, 1] = (sums[h, 1] + gz_recv[h, 0].astype(F32)).astype(BF16)
+
+        @pl.when(c >= 2)
+        def _():
+            front_copy(h, 1).start()
 
     for r in range(1, n_dp):
         kv_copy(r).start()
@@ -269,11 +343,15 @@
         turned = rotate(unit * gk_t[...], cos_ref[...], sin_ref[...])
         ring_send[h, :, :d] = turned.T.astype(BF16)
         ring_send[h, :, d:] = kv_recv[:, kw + h * d : kw + (h + 1) * d]
-        for s in range(1, blocks):
-
-            @pl.when((c + s < n_cp) & (h < ahead))
-            def _():
-                ring_copy(h, s).start()
+        for plan in ring_plan(h)[:2]:
+            start_if(plan)
+    for h in range(kv):
+        ring_arrived(h, 2)
+        for plan in ring_plan(h)[2:5]:
+            start_if(plan)
+    for h in range(kv):
+        ring_arrived(h, 4)
+        start_if(ring_plan(h)[5])
 
     def out_copy(h, src, dst, which):
         return pltpu.make_async_copy(
@@ -285,22 +363,13 @@
     def head(h, carry):
         for r in range(1, n_dp):
             qg_copy(h, r).wait_recv()
-        for s in range(1, blocks):
-
-            @pl.when(c >= s)
-            def _():
-                ring_copy(h, s).wait_recv()
+        ring_arrived(h, 1)
+        ring_arrived(h, 3)
 
         @pl.when(h + ahead < kv)
         def _():
             for r in range(1, n_dp):
                 qg_copy(h + ahead, r).start()
-        for s in range(1, blocks):
-
-            @pl.when((c + s < n_cp) & (h + ahead < kv))
-            def _():
-                ring_copy(h + ahead, s).start()
-
         for s in range(blocks):
             both = ring_send[h] if s == 0 else ring_recv[h, s - 1]
             keys[s * tok : (s + 1) * tok, :] = both[:, :d]
@@ -329,7 +398,7 @@
             for s in range(1, blocks):
                 top = jnp.maximum(top, jnp.max(parts[s], axis=0, keepdims=True) - away[s - 1])
             weights = [
-                jnp.exp2((parts[s] - (top if s == 0 else top + away[s - 1])) * exp_scale)
+                jnp.exp((parts[s] - (top if s == 0 else top + away[s - 1])) * inv_root)
                 for s in range(blocks)
             ]
             weights = jnp.concatenate(weights, axis=0)
@@ -350,36 +419,47 @@
             return carry
 
         lax.fori_loop(0, grp // pair, some, 0)
-        for s in range(1, blocks):
+        for s in range(blocks):
             at = slice(s * tok, (s + 1) * tok)
-            grad_send[h, s - 1, :, :d] = (dk_own[at, :] * inv_root).astype(BF16)
-            grad_send[h, s - 1, :, d:] = dv_own[at, :].astype(BF16)
-
-            @pl.when(c >= s)
-            def _():
-                grad_copy(h, s).start()
-
-        dk_sum[h] = dk_own[:tok, :] * inv_root
-        dv_sum[h] = dv_own[:tok, :]
+            if s % 2 == 1:
+                grad_send[h, s - 1, :, :d] = (dk_own[at, :] * inv_root).astype(BF16)
+                grad_send[h, s - 1, :, d:] = dv_own[at, :].astype(BF16)
+
+                @pl.when(c >= s)
+                def _():
+                    mate_copy(h, s // 2).start()
+
+            else:
+                sums[h, s // 2, :, :d] = dk_own[at, :] * inv_root
+                sums[h, s // 2, :, d:] = dv_own[at, :]
+
+        @pl.when(h >= 1)
+        def _():
+            after_mate(h - 1)
+
+        @pl.when(h >= 2)
+        def _():
+            after_four(h - 2)
+
         out_copy(h, out_buf, out_hbm, 0).start()
         out_copy(h, dq_buf, dq_hbm, 1).start()
         return carry
 
     lax.fori_loop(0, kv, head, 0)
+    after_mate(kv - 1)
+    if kv >= 2:
+        after_four(kv - 2)
+    after_four(kv - 1)
 
     acc_k = jnp.zeros((d, tok), F32)
     for h in range(kv):
-        for s in range(1, blocks):
-
-            @pl.when(c + s < n_cp)
-            def _():
-                grad_copy(h, s).wait_recv()
-
-        dk = dk_sum[h]
-        dv = dv_sum[h]
-        for s in range(1, blocks):
-            dk = dk + grad_recv[h, s - 1, :, :d].astype(F32)
-            dv = dv + grad_recv[h, s - 1, :, d:].astype(F32)
+
+        @pl.when(c + 2 < n_cp)
+        def _():
+            front_copy(h, 1).wait_recv()
+
+        both = sums[h, 0] + gz_recv[h, 1].astype(F32)
+        dk, dv = both[:, :d], both[:, d:]
         at = slice(h * d, (h + 1) * d)
         dv_ref[:, at] = dv.astype(BF16)
         dkn = unrotate(dk.T, cos_ref[...], sin_ref[...])
@@ -447,15 +527,21 @@
     def settle(h, carry):
         for r in range(1, n_dp):
             qg_copy(h, r).wait_send()
-        for s in range(1, blocks):
-
-            @pl.when(c + s < n_cp)
+        for copy, wanted in ring_plan(h):
+
+            @pl.when(wanted)
             def _():
-                ring_copy(h, s).wait_send()
-
-            @pl.when(c >= s)
+                copy.wait_send()
+
+        for i in range(2):
+
+            @pl.when(c >= 1 + 2 * i)
             def _():
-                grad_copy(h, s).wait_send()
+                mate_copy(h, i).wait_send()
+
+            @pl.when(c >= 4 - 2 * i)
+            def _():
+                front_copy(h, i).wait_send()
 
         out_copy(h, out_buf, out_hbm, 0).wait()
         out_copy(h, dq_buf, dq_hbm, 1).wait()
@@ -468,15 +554,34 @@
     gains_ref[...] = total
 
 
-def hand_out(out, dq, dk, dv, gains, out_o, dq_o, dk_o, dv_o, gq_o, gk_o, sem):
-    pairs = [
-        (out, out_o), (dq, dq_o), (dk, dk_o), (dv, dv_o),
-        (gains.at[0:1], gq_o), (gains.at[1:2], gk_o),
+def hand_out(
+    out, dq, dk, dv, gains, out_o, dq_o, dk_o, dv_o, gq_o, gk_o,
+    out_v, dq_v, dk_v, dv_v, in_sem, out_sem,
+):
+    half = out.shape[0] // 2
+    plan = [
+        (ref.at[at], held.at[at], final.at[at])
+        for ref, held, final in ((out, out_v, out_o), (dq, dq_v, dq_o))
+        for at in (pl.ds(0, half), pl.ds(half, half))
+    ] + [(dk, dk_v, dk_o), (dv, dv_v, dv_o)]
+    into = [
+        pltpu.make_async_copy(ref, held, in_sem.at[i]) for i, (ref, held, _) in enumerate(plan)
     ]
-    copies = [pltpu.make_async_copy(src, dst, sem.at[i]) for i, (src, dst) in enumerate(pairs)]
-    for copy in copies:
+    away = [
+        pltpu.make_async_copy(held, final, out_sem.at[i]) for i, (_, held, final) in enumerate(plan)
+    ]
+    for copy in into:
         copy.start()
-    for copy in copies:
+    last = [
+        pltpu.make_async_copy(gains.at[0:1], gq_o, out_sem.at[6]),
+        pltpu.make_async_copy(gains.at[1:2], gk_o, out_sem.at[7]),
+    ]
+    for copy in last:
+        copy.start()
+    for there, copy in zip(into, away):
+        there.wait()
+        copy.start()
+    for copy in away + last:
         copy.wait()
 
 
@@ -489,7 +594,7 @@
     blocks = min(MOST_BLK, n_cp)
     reach = blocks - 1
     pair = 4 if grp % 4 == 0 else 1
-    assert doc_blocks.shape == (1, 1)
+    assert doc_blocks.shape == (1, 1) and n_cp % 2 == 0 and n_cp >= 6 and MOST_BLK == 5
     frequency = THETA ** (-(np.arange(d // 2, dtype=np.float64) * 2.0 / d))
     angles = frequency[:, None] * np.arange(MOST_BLK * tok, dtype=np.float64)[None, :]
     table = jnp.asarray(np.concatenate([np.cos(angles), np.sin(angles)]).astype(np.float32))
@@ -532,11 +637,11 @@
             V((d, blocks * tok), BF16),
             V((d, blocks * tok), BF16),
             V((kv, reach, tok, 2 * d), BF16),
-            V((kv, reach, tok, 2 * d), BF16),
+            V((kv, 2, tok, 2 * d), BF16),
+            V((kv, 2, tok, 2 * d), BF16),
             V((blocks * tok, d), F32),
             V((blocks * tok, d), F32),
-            V((kv, tok, d), F32),
-            V((kv, tok, d), F32),
+            V((kv, 3, tok, 2 * d), F32),
             V((kv, d, tok), F32),
             V((kv, 8, tok), F32),
             V((d // 2, tok), F32),
@@ -560,10 +665,12 @@
             dma((kv, n_dp - 1)),
             dma((reach,)),
             dma((reach,)),
+            dma((kv, 4)),
             dma((kv, reach)),
-            dma((kv, reach)),
-            dma((kv, reach)),
-            dma((kv, reach)),
+            dma((kv, 2)),
+            dma((kv, 2)),
+            dma((kv, 2)),
+            dma((kv, 2)),
             dma((n_dp - 1,)),
             dma((n_dp - 1,)),
             dma((n_cp - 1,)),
@@ -582,7 +689,7 @@
         + [jax.ShapeDtypeStruct((1, d), F32)] * 2,
         in_specs=[anywhere] * 4 + [vmem],
         out_specs=[hbm] * 6,
-        scratch_shapes=[dma((6,))],
+        scratch_shapes=[V(x.shape, x.dtype) for x in outs[:4]] + [dma((6,)), dma((8,))],
         compiler_params=pltpu.CompilerParams(vmem_limit_bytes=60 * 1024 * 1024),
     )(*outs)
     return (*outs[:4], outs[4].reshape(d), outs[5].reshape(d))

time: 142 us -> 63.7 us (0.45)
  Pallas kernels: 141 us -> 62.2 us
    pallas_call x1, Pallas kernels: 73.3 us -> 3.24 us  [body(): pl.pallas_call(hand_out, out_shape=[jax.ShapeDtypeStruct(x.shape, x.dtype...]
    pallas_call x1, Pallas kernels: 67.5 us -> 59 us  [body(): pl.pallas_call(functools.partial(kernel, n_dp, n_cp, kv, grp, d, tok, pai...]
where the time goes in v2:
time: 63.7 us; the launch traced here: 63.5 us
  Pallas kernels  62.2 us (98%)
  between operations  1.29 us (2%)
    pallas_call x1, Pallas kernels, body(): pl.pallas_call(functools.partial(kernel, n_dp, n_cp, kv, grp, d, tok, pai...  59 us
    pallas_call x1, Pallas kernels, body(): pl.pallas_call(hand_out, out_shape=[jax.ShapeDtypeStruct(x.shape, x.dtype...  3.24 us

profile of v2, /device:TPU:0, one launch (start us, length us, event | category | flops | bytes accessed | tf_op | source)
XLA Modules:
  0.0 63.5 jit_solution(13133540274901504358)
XLA Ops:
  1.3 59.0 %shard_map.136 = (bf16[128,4096]{1,0:T(8,128)(2,1)}, bf16[128,4096]{1,0:T(8,128)(2,1)}, bf16[128,512]{1,0:T(8,128)(2,1)}, bf16[128,512]{1,0:T(8,128)(2,1)}, f32[8,128]{1,0:T(8,128)}) custom-call(bf16[128,4096]{1,0:T(8,128)(2,1)} %q_hbm.1, bf16[128,512]{1,0:T(8,128)(2,1)} %k_hbm.1, bf16[128,512]{1,0:T(8,128)(2,1)} %v_hbm.1, bf16[128,4096]{1,0:T(8,128)(2,1)} %g_hbm.1, ...), custom_call_target="tpu_custom_call" | custom-call | tf_op jit(solution)/shard_map/pallas_call | solution.py:606
  60.3 3.2 %shard_map.137 = (bf16[128,4096]{1,0:T(8,128)(2,1)}, bf16[128,4096]{1,0:T(8,128)(2,1)}, bf16[128,512]{1,0:T(8,128)(2,1)}, bf16[128,512]{1,0:T(8,128)(2,1)}, f32[1,128]{1,0:T(1,128)}, /*index=5*/f32[1,128]{1,0:T(1,128)}) custom-call(bf16[128,4096]{1,0:T(8,128)(2,1)} %get-tuple-element.17.out, bf16[128,4096]{1,0:T(8,128)(2,1)} %get-tuple-element.18.dq, ...), custom_call_target="tpu_custom_call" | custom-call | tf_op jit(solution)/shard_map/pallas_call | solution.py:686

commit v3 on v2

--- a/solution.py
+++ b/solution.py
@@ -64,7 +64,7 @@
     out_hbm, dq_hbm, dk_ref, dv_ref, gains_ref,
     q_in, k_in, v_in, g_in, order_ref, gq_ref, gk_ref, table_ref, hot, kv_send, kv_recv, qg_send, qg_recv,
     id_send, id_recv, ring_send, ring_recv, keys, vals, keys_t, vals_t,
-    grad_send, gy_recv, gz_recv, dk_own, dv_own, sums, k_unit, k_inv,
+    grad_send, gy_recv, gz_recv, dk_own, dv_own, sums, held, units, invs, k_unit, k_inv,
     cos_ref, sin_ref, gq_t, gk_t, tri, out_buf, dq_buf, acc_q, part, tot, dp_recv, cp_recv,
     small_sem, in_sem, out_sem, kvs_sem, kvr_sem, qgs_sem, qgr_sem, ids_sem, idr_sem,
     rs_sem, rr_sem, gys_sem, gyr_sem, gzs_sem, gzr_sem, ds_sem, dr_sem, cs_sem, cr_sem,
@@ -73,7 +73,11 @@
     c = lax.axis_index("cp")
     reach = min(MOST_BLK - 1, n_cp - 1)
     blocks = reach + 1
-    ahead = min(3, kv)
+    per = grp // pair
+    shares = kv * per
+    early = min(2, kv)
+    ahead = min(5, shares)
+    span = pair * d
     even = lax.rem(c, 2) == 0
     even_f = even.astype(F32)
     mate = c + 1 - 2 * lax.rem(c, 2)
@@ -179,13 +183,13 @@
             device_id_type=MESH,
         )
 
-    def qg_copy(h, r):
+    def qg_copy(i, r):
         peer = lax.rem(a + r, n_dp)
         return pltpu.make_async_remote_copy(
-            src_ref=qg_send.at[h, pl.ds(pl.multiple_of(peer * rows, rows), rows), :],
-            dst_ref=qg_recv.at[h, mine, :],
-            send_sem=qgs_sem.at[h, r - 1],
-            recv_sem=qgr_sem.at[h, r - 1],
+            src_ref=qg_send.at[i, pl.ds(pl.multiple_of(peer * rows, rows), rows), :],
+            dst_ref=qg_recv.at[i, mine, :],
+            send_sem=qgs_sem.at[i, r - 1],
+            recv_sem=qgr_sem.at[i, r - 1],
             device_id={"dp": peer},
             device_id_type=MESH,
         )
@@ -236,6 +240,19 @@
         def _():
             copy.start()
 
+    def ring_begin(h):
+        for plan in ring_plan(h)[:2]:
+            start_if(plan)
+
+    def ring_pass(h):
+        ring_arrived(h, 2)
+        for plan in ring_plan(h)[2:5]:
+            start_if(plan)
+
+    def ring_end(h):
+        ring_arrived(h, 4)
+        start_if(ring_plan(h)[5])
+
     def mate_copy(h, i):
         return pltpu.make_async_remote_copy(
             src_ref=grad_send.at[h, 2 * i],
@@ -292,21 +309,24 @@
         def _():
             id_copy(s).start()
 
-    def gather(h, carry):
-        in_copy(h, q_hbm, q_in, 0).wait()
-        in_copy(h, g_hbm, g_in, 1).wait()
-        qg_send[h, :, :width] = dot(hot[...], q_in[:, columns(h, width)]).astype(BF16)
-        qg_send[h, :, width:] = dot(hot[...], g_in[:, columns(h, width)]).astype(BF16)
-        qg_recv[h, mine, :] = qg_send[h, mine, :]
-
-        @pl.when(h < ahead)
+    def gather(i, carry):
+        @pl.when(lax.rem(i, per) == 0)
+        def _():
+            in_copy(i // per, q_hbm, q_in, 0).wait()
+            in_copy(i // per, g_hbm, g_in, 1).wait()
+
+        qg_send[i, :, :span] = dot(hot[...], q_in[:, columns(i, span)]).astype(BF16)
+        qg_send[i, :, span:] = dot(hot[...], g_in[:, columns(i, span)]).astype(BF16)
+        qg_recv[i, mine, :] = qg_send[i, mine, :]
+
+        @pl.when(i < ahead)
         def _():
             for r in range(1, n_dp):
-                qg_copy(h, r).start()
+                qg_copy(i, r).start()
 
         return carry
 
-    lax.fori_loop(0, kv, gather, 0)
+    lax.fori_loop(0, shares, gather, 0)
 
     for s in range(1, blocks):
 
@@ -343,33 +363,23 @@
         turned = rotate(unit * gk_t[...], cos_ref[...], sin_ref[...])
         ring_send[h, :, :d] = turned.T.astype(BF16)
         ring_send[h, :, d:] = kv_recv[:, kw + h * d : kw + (h + 1) * d]
-        for plan in ring_plan(h)[:2]:
-            start_if(plan)
-    for h in range(kv):
-        ring_arrived(h, 2)
-        for plan in ring_plan(h)[2:5]:
-            start_if(plan)
-    for h in range(kv):
-        ring_arrived(h, 4)
-        start_if(ring_plan(h)[5])
+        if h < early:
+            ring_begin(h)
+    for h in range(early):
+        ring_pass(h)
+    for h in range(early, kv):
+        ring_begin(h)
+    for h in range(early):
+        ring_end(h)
 
     def out_copy(h, src, dst, which):
         return pltpu.make_async_copy(
             src.at[:, columns(h, width)], dst.at[:, columns(h, width)], out_sem.at[which, h]
         )
 
-    span = pair * d
-
     def head(h, carry):
-        for r in range(1, n_dp):
-            qg_copy(h, r).wait_recv()
         ring_arrived(h, 1)
         ring_arrived(h, 3)
-
-        @pl.when(h + ahead < kv)
-        def _():
-            for r in range(1, n_dp):
-                qg_copy(h + ahead, r).start()
         for s in range(blocks):
             both = ring_send[h] if s == 0 else ring_recv[h, s - 1]
             keys[s * tok : (s + 1) * tok, :] = both[:, :d]
@@ -380,16 +390,31 @@
         dv_own[...] = jnp.zeros_like(dv_own)
 
         def some(j, carry):
+            i = h * per + j
+            for r in range(1, n_dp):
+                qg_copy(i, r).wait_recv()
+
+            @pl.when(i + ahead < shares)
+            def _():
+                for r in range(1, n_dp):
+                    qg_copy(i + ahead, r).start()
+
+            @pl.when(i == 1)
+            def _():
+                for later in range(early, kv):
+                    ring_pass(later)
+
             cos = wide(cos_ref[...], pair)
             sin = wide(sin_ref[...], pair)
             gain = wide(gq_t[...], pair)
-            unit, inv = unit_of(flip(qg_recv[h, :, columns(j, span)], d).astype(F32))
+            unit, inv = unit_of(flip(qg_recv[i, :, :span], d).astype(F32))
+            units[j] = unit
+            invs[j] = jnp.broadcast_to(inv, (8, span))
             turned = rotate(unit * gain, cos, sin).astype(BF16)
-            g_at = pl.ds(pl.multiple_of(width + j * span, span), span)
-            g_rows = qg_recv[h, :, g_at]
+            g_rows = qg_recv[i, :, span:]
             g_t = flip(g_rows, d)
             g_rows = jnp.concatenate(
-                [g_rows[:, i * d : (i + 1) * d] for i in range(pair)], axis=0
+                [g_rows[:, at : at + d] for at in range(0, span, d)], axis=0
             )
             scores = dot(keys[...], turned)
             parts = [scores[s * tok : (s + 1) * tok] for s in range(blocks)]
@@ -410,15 +435,11 @@
             dscores = (probs * (dprobs - delta)).astype(BF16)
             dk_own[...] += dot_nt(dscores, turned)
             dv_own[...] += dot(probs.astype(BF16), g_rows)
-            dqn = unrotate(dot(keys_t[...], dscores) * inv_root, cos, sin)
-            term = dqn * unit
-            acc_q[...] += sum(term[:, i * d : (i + 1) * d] for i in range(pair))
-            at = pl.ds(pl.multiple_of(h * width + j * span, span), span)
-            out_buf[:, at] = flip(out_t, d)
-            dq_buf[:, at] = flip(norm_back(dqn, unit, inv, gain).astype(BF16), d)
+            held[j] = dscores
+            out_buf[:, columns(i, span)] = flip(out_t, d)
             return carry
 
-        lax.fori_loop(0, grp // pair, some, 0)
+        lax.fori_loop(0, per, some, 0)
         for s in range(blocks):
             at = slice(s * tok, (s + 1) * tok)
             if s % 2 == 1:
@@ -432,6 +453,24 @@
             else:
                 sums[h, s // 2, :, :d] = dk_own[at, :] * inv_root
                 sums[h, s // 2, :, d:] = dv_own[at, :]
+
+        @pl.when(h == 0)
+        def _():
+            for later in range(early, kv):
+                ring_end(later)
+
+        def query_grads(j, carry):
+            cos = wide(cos_ref[...], pair)
+            sin = wide(sin_ref[...], pair)
+            unit = units[j]
+            dqn = unrotate(dot(keys_t[...], held[j]) * inv_root, cos, sin)
+            term = dqn * unit
+            acc_q[...] += sum(term[:, at : at + d] for at in range(0, span, d))
+            grads = norm_back(dqn, unit, invs[j, 0:1, :], wide(gq_t[...], pair))
+            dq_buf[:, columns(h * per + j, span)] = flip(grads.astype(BF16), d)
+            return carry
+
+        lax.fori_loop(0, per, query_grads, 0)
 
         @pl.when(h >= 1)
         def _():
@@ -525,8 +564,9 @@
             id_copy(s).wait_send()
 
     def settle(h, carry):
-        for r in range(1, n_dp):
-            qg_copy(h, r).wait_send()
+        for j in range(per):
+            for r in range(1, n_dp):
+                qg_copy(h * per + j, r).wait_send()
         for copy, wanted in ring_plan(h):
 
             @pl.when(wanted)
@@ -593,7 +633,8 @@
     grp = q_width // kw
     blocks = min(MOST_BLK, n_cp)
     reach = blocks - 1
-    pair = 4 if grp % 4 == 0 else 1
+    pair = 4 if grp % 8 == 0 else 1
+    per = grp // pair
     assert doc_blocks.shape == (1, 1) and n_cp % 2 == 0 and n_cp >= 6 and MOST_BLK == 5
     frequency = THETA ** (-(np.arange(d // 2, dtype=np.float64) * 2.0 / d))
     angles = frequency[:, None] * np.arange(MOST_BLK * tok, dtype=np.float64)[None, :]
@@ -626,8 +667,8 @@
             V((tok, tok), BF16),
             V((tok, 2 * kw), BF16),
             V((tok, 2 * kw), BF16),
-            V((kv, tok, 2 * grp * d), BF16),
-            V((kv, tok, 2 * grp * d), BF16),
+            V((kv * per, tok, 2 * pair * d), BF16),
+            V((kv * per, tok, 2 * pair * d), BF16),
             V((8, 128), jnp.int32),
             V((reach, 8, 128), jnp.int32),
             V((kv, tok, 2 * d), BF16),
@@ -642,6 +683,9 @@
             V((blocks * tok, d), F32),
             V((blocks * tok, d), F32),
             V((kv, 3, tok, 2 * d), F32),
+            V((per, blocks * tok, pair * d), BF16),
+            V((per, d, pair * d), F32),
+            V((per, 8, pair * d), F32),
             V((kv, d, tok), F32),
             V((kv, 8, tok), F32),
             V((d // 2, tok), F32),
@@ -661,8 +705,8 @@
             dma((2, kv)),
             dma((n_dp - 1,)),
             dma((n_dp - 1,)),
-            dma((kv, n_dp - 1)),
-            dma((kv, n_dp - 1)),
+            dma((kv * per, n_dp - 1)),
+            dma((kv * per, n_dp - 1)),
             dma((reach,)),
             dma((reach,)),
             dma((kv, 4)),

time: 63.7 us -> 63.5 us (level)
  no operation moved by 1% of the time
where the time goes in v3:
time: 63.5 us; the launch traced here: 63.3 us
  Pallas kernels  62 us (98%)
  between operations  1.29 us (2%)
    pallas_call x1, Pallas kernels, body(): pl.pallas_call(functools.partial(kernel, n_dp, n_cp, kv, grp, d, tok, pai...  58.8 us
    pallas_call x1, Pallas kernels, body(): pl.pallas_call(hand_out, out_shape=[jax.ShapeDtypeStruct(x.shape, x.dtype...  3.24 us

profile of v3, /device:TPU:0, one launch (start us, length us, event | category | flops | bytes accessed | tf_op | source)
XLA Modules:
  0.0 63.3 jit_solution(17594861971931131236)
XLA Ops:
  1.3 58.8 %shard_map.136 = (bf16[128,4096]{1,0:T(8,128)(2,1)}, bf16[128,4096]{1,0:T(8,128)(2,1)}, bf16[128,512]{1,0:T(8,128)(2,1)}, bf16[128,512]{1,0:T(8,128)(2,1)}, f32[8,128]{1,0:T(8,128)}) custom-call(bf16[128,4096]{1,0:T(8,128)(2,1)} %q_hbm.1, bf16[128,512]{1,0:T(8,128)(2,1)} %k_hbm.1, bf16[128,512]{1,0:T(8,128)(2,1)} %v_hbm.1, bf16[128,4096]{1,0:T(8,128)(2,1)} %g_hbm.1, ...), custom_call_target="tpu_custom_call" | custom-call | tf_op jit(solution)/shard_map/pallas_call | solution.py:647
  60.1 3.2 %shard_map.137 = (bf16[128,4096]{1,0:T(8,128)(2,1)}, bf16[128,4096]{1,0:T(8,128)(2,1)}, bf16[128,512]{1,0:T(8,128)(2,1)}, bf16[128,512]{1,0:T(8,128)(2,1)}, f32[1,128]{1,0:T(1,128)}, /*index=5*/f32[1,128]{1,0:T(1,128)}) custom-call(bf16[128,4096]{1,0:T(8,128)(2,1)} %get-tuple-element.17.out, bf16[128,4096]{1,0:T(8,128)(2,1)} %get-tuple-element.18.dq, ...), custom_call_target="tpu_custom_call" | custom-call | tf_op jit(solution)/shard_map/pallas_call | solution.py:730

commit v4 on v3

--- a/solution.py
+++ b/solution.py
@@ -61,12 +61,12 @@
 def kernel(
     n_dp, n_cp, kv, grp, d, tok, pair,
     q_hbm, k_hbm, v_hbm, g_hbm, order_hbm, doc_ref, gq_hbm, gk_hbm, table_hbm,
-    out_hbm, dq_hbm, dk_ref, dv_ref, gains_ref,
+    out_buf, dq_buf, dk_ref, dv_ref, gains_ref,
     q_in, k_in, v_in, g_in, order_ref, gq_ref, gk_ref, table_ref, hot, kv_send, kv_recv, qg_send, qg_recv,
     id_send, id_recv, ring_send, ring_recv, keys, vals, keys_t, vals_t,
     grad_send, gy_recv, gz_recv, dk_own, dv_own, sums, held, units, invs, k_unit, k_inv,
-    cos_ref, sin_ref, gq_t, gk_t, tri, out_buf, dq_buf, acc_q, part, tot, dp_recv, cp_recv,
-    small_sem, in_sem, out_sem, kvs_sem, kvr_sem, qgs_sem, qgr_sem, ids_sem, idr_sem,
+    cos_ref, sin_ref, gq_t, gk_t, tri, acc_q, part, tot, dp_recv, cp_recv,
+    small_sem, in_sem, kvs_sem, kvr_sem, qgs_sem, qgr_sem, ids_sem, idr_sem,
     rs_sem, rr_sem, gys_sem, gyr_sem, gzs_sem, gzr_sem, ds_sem, dr_sem, cs_sem, cr_sem,
 ):
     a = lax.axis_index("dp")
@@ -371,11 +371,6 @@
         ring_begin(h)
     for h in range(early):
         ring_end(h)
-
-    def out_copy(h, src, dst, which):
-        return pltpu.make_async_copy(
-            src.at[:, columns(h, width)], dst.at[:, columns(h, width)], out_sem.at[which, h]
-        )
 
     def head(h, carry):
         ring_arrived(h, 1)
@@ -480,18 +475,16 @@
         def _():
             after_four(h - 2)
 
-        out_copy(h, out_buf, out_hbm, 0).start()
-        out_copy(h, dq_buf, dq_hbm, 1).start()
         return carry
 
     lax.fori_loop(0, kv, head, 0)
     after_mate(kv - 1)
     if kv >= 2:
         after_four(kv - 2)
-    after_four(kv - 1)
-
     acc_k = jnp.zeros((d, tok), F32)
     for h in range(kv):
+        if h == max(kv - 2, 0):
+            after_four(kv - 1)
 
         @pl.when(c + 2 < n_cp)
         def _():
@@ -583,8 +576,6 @@
             def _():
                 front_copy(h, i).wait_send()
 
-        out_copy(h, out_buf, out_hbm, 0).wait()
-        out_copy(h, dq_buf, dq_hbm, 1).wait()
         return carry
 
     lax.fori_loop(0, kv, settle, 0)
@@ -594,34 +585,15 @@
     gains_ref[...] = total
 
 
-def hand_out(
-    out, dq, dk, dv, gains, out_o, dq_o, dk_o, dv_o, gq_o, gk_o,
-    out_v, dq_v, dk_v, dv_v, in_sem, out_sem,
-):
-    half = out.shape[0] // 2
-    plan = [
-        (ref.at[at], held.at[at], final.at[at])
-        for ref, held, final in ((out, out_v, out_o), (dq, dq_v, dq_o))
-        for at in (pl.ds(0, half), pl.ds(half, half))
-    ] + [(dk, dk_v, dk_o), (dv, dv_v, dv_o)]
-    into = [
-        pltpu.make_async_copy(ref, held, in_sem.at[i]) for i, (ref, held, _) in enumerate(plan)
+def hand_out(out, dq, dk, dv, gains, out_o, dq_o, dk_o, dv_o, gq_o, gk_o, sem):
+    pairs = [
+        (out, out_o), (dq, dq_o), (dk, dk_o), (dv, dv_o),
+        (gains.at[0:1], gq_o), (gains.at[1:2], gk_o),
     ]
-    away = [
-        pltpu.make_async_copy(held, final, out_sem.at[i]) for i, (_, held, final) in enumerate(plan)
-    ]
-    for copy in into:
+    copies = [pltpu.make_async_copy(src, dst, sem.at[i]) for i, (src, dst) in enumerate(pairs)]
+    for copy in copies:
         copy.start()
-    last = [
-        pltpu.make_async_copy(gains.at[0:1], gq_o, out_sem.at[6]),
-        pltpu.make_async_copy(gains.at[1:2], gk_o, out_sem.at[7]),
-    ]
-    for copy in last:
-        copy.start()
-    for there, copy in zip(into, away):
-        there.wait()
-        copy.start()
-    for copy in away + last:
+    for copy in copies:
         copy.wait()
 
 
@@ -641,20 +613,19 @@
     table = jnp.asarray(np.concatenate([np.cos(angles), np.sin(angles)]).astype(np.float32))
     vmem = pl.BlockSpec(memory_space=pltpu.VMEM)
     hbm = pl.BlockSpec(memory_space=pltpu.HBM)
-    anywhere = pl.BlockSpec(memory_space=pl.ANY)
     dma = pltpu.SemaphoreType.DMA
     V = pltpu.VMEM
     outs = pl.pallas_call(
         functools.partial(kernel, n_dp, n_cp, kv, grp, d, tok, pair),
         out_shape=[
-            jax.ShapeDtypeStruct((tok, q_width), BF16),
-            jax.ShapeDtypeStruct((tok, q_width), BF16),
-            jax.ShapeDtypeStruct((tok, kw), BF16),
-            jax.ShapeDtypeStruct((tok, kw), BF16),
-            jax.ShapeDtypeStruct((8, d), F32),
+            V((tok, q_width), BF16),
+            V((tok, q_width), BF16),
+            V((tok, kw), BF16),
+            V((tok, kw), BF16),
+            V((8, d), F32),
         ],
         in_specs=[hbm] * 5 + [vmem] + [hbm] * 3,
-        out_specs=[anywhere] * 2 + [vmem] * 3,
+        out_specs=[vmem] * 5,
         scratch_shapes=[
             V((tok, q_width), BF16),
             V((tok, kw), BF16),
@@ -693,8 +664,6 @@
             V((d, d), F32),
             V((d, d), F32),
             V((tok, tok), F32),
-            V((tok, q_width), BF16),
-            V((tok, q_width), BF16),
             V((d, tok), F32),
             V((8, d), F32),
             V((8, d), F32),
@@ -702,7 +671,6 @@
             V((n_cp, 8, d), F32),
             dma((4,)),
             dma((4, kv)),
-            dma((2, kv)),
             dma((n_dp - 1,)),
             dma((n_dp - 1,)),
             dma((kv * per, n_dp - 1)),
@@ -721,7 +689,7 @@
             dma((n_cp - 1,)),
         ],
         compiler_params=pltpu.CompilerParams(
-            collective_id=0, has_side_effects=True, vmem_limit_bytes=60 * 1024 * 1024
+            collective_id=0, has_side_effects=True, vmem_limit_bytes=56 * 1024 * 1024
         ),
     )(
         q_raw, k_raw, values, loss_grad, send_order, doc_blocks,
@@ -731,10 +699,10 @@
         hand_out,
         out_shape=[jax.ShapeDtypeStruct(x.shape, x.dtype) for x in outs[:4]]
         + [jax.ShapeDtypeStruct((1, d), F32)] * 2,
-        in_specs=[anywhere] * 4 + [vmem],
+        in_specs=[vmem] * 5,
         out_specs=[hbm] * 6,
-        scratch_shapes=[V(x.shape, x.dtype) for x in outs[:4]] + [dma((6,)), dma((8,))],
-        compiler_params=pltpu.CompilerParams(vmem_limit_bytes=60 * 1024 * 1024),
+        scratch_shapes=[dma((6,))],
+        compiler_params=pltpu.CompilerParams(vmem_limit_bytes=8 * 1024 * 1024),
     )(*outs)
     return (*outs[:4], outs[4].reshape(d), outs[5].reshape(d))
 

time: 63.5 us -> 60.8 us (0.957)
  Pallas kernels: 62 us -> 59.4 us
    pallas_call x1, Pallas kernels: 3.24 us -> 1.45 us  [body(): pl.pallas_call(hand_out, out_shape=[jax.ShapeDtypeStruct(x.shape, x.dtype...]
    pallas_call x1, Pallas kernels: 58.8 us -> 57.9 us  [body(): pl.pallas_call(functools.partial(kernel, n_dp, n_cp, kv, grp, d, tok, pai...]
where the time goes in v4:
time: 60.8 us; the launch traced here: 60.7 us
  Pallas kernels  59.4 us (98%)
  between operations  1.29 us (2%)
    pallas_call x1, Pallas kernels, body(): pl.pallas_call(functools.partial(kernel, n_dp, n_cp, kv, grp, d, tok, pai...  57.9 us
    pallas_call x1, Pallas kernels, body(): pl.pallas_call(hand_out, out_shape=[jax.ShapeDtypeStruct(x.shape, x.dtype...  1.45 us

profile of v4, /device:TPU:0, one launch (start us, length us, event | category | flops | bytes accessed | tf_op | source)
XLA Modules:
  0.0 60.7 jit_solution(1260558203429940016)
XLA Ops:
  1.3 57.9 %shard_map.136 = (bf16[128,4096]{1,0:T(8,128)(2,1)S(1)}, bf16[128,4096]{1,0:T(8,128)(2,1)S(1)}, bf16[128,512]{1,0:T(8,128)(2,1)S(1)}, bf16[128,512]{1,0:T(8,128)(2,1)S(1)}, f32[8,128]{1,0:T(8,128)S(1)}) custom-call(bf16[128,4096]{1,0:T(8,128)(2,1)} %q_hbm.1, bf16[128,512]{1,0:T(8,128)(2,1)} %k_hbm.1, bf16[128,512]{1,0:T(8,128)(2,1)} %v_hbm.1, ...), custom_call_target="tpu_custom_call" | custom-call | tf_op jit(solution)/shard_map/pallas_call | solution.py:618
  59.2 1.4 %shard_map.137 = (bf16[128,4096]{1,0:T(8,128)(2,1)}, bf16[128,4096]{1,0:T(8,128)(2,1)}, bf16[128,512]{1,0:T(8,128)(2,1)}, bf16[128,512]{1,0:T(8,128)(2,1)}, f32[1,128]{1,0:T(1,128)}, /*index=5*/f32[1,128]{1,0:T(1,128)}) custom-call(bf16[128,4096]{1,0:T(8,128)(2,1)S(1)} %get-tuple-element.17.out, bf16[128,4096]{1,0:T(8,128)(2,1)S(1)} %get-tuple-element.18.dq, ...), custom_call_target="tpu_custom_call" | custom-call | tf_op jit(solution)/shard_map/pallas_call | solution.py:698

commit v5 on v4

--- a/solution.py
+++ b/solution.py
@@ -76,7 +76,7 @@
     per = grp // pair
     shares = kv * per
     early = min(2, kv)
-    ahead = min(5, shares)
+    ahead = min(3, shares)
     span = pair * d
     even = lax.rem(c, 2) == 0
     even_f = even.astype(F32)
@@ -309,6 +309,10 @@
         def _():
             id_copy(s).start()
 
+    def send_share(i):
+        for r in range(1, n_dp):
+            qg_copy(i, r).start()
+
     def gather(i, carry):
         @pl.when(lax.rem(i, per) == 0)
         def _():
@@ -319,10 +323,9 @@
         qg_send[i, :, span:] = dot(hot[...], g_in[:, columns(i, span)]).astype(BF16)
         qg_recv[i, mine, :] = qg_send[i, mine, :]
 
-        @pl.when(i < ahead)
-        def _():
-            for r in range(1, n_dp):
-                qg_copy(i, r).start()
+        @pl.when(i == 0)
+        def _():
+            send_share(0)
 
         return carry
 
@@ -354,6 +357,8 @@
 
     for r in range(1, n_dp):
         kv_copy(r).wait_recv()
+    if ahead > 1:
+        send_share(1)
 
     for h in range(kv):
         x = kv_recv[:, h * d : (h + 1) * d].astype(F32).T
@@ -367,6 +372,8 @@
             ring_begin(h)
     for h in range(early):
         ring_pass(h)
+    for i in range(2, ahead):
+        send_share(i)
     for h in range(early, kv):
         ring_begin(h)
     for h in range(early):
@@ -391,8 +398,7 @@
 
             @pl.when(i + ahead < shares)
             def _():
-                for r in range(1, n_dp):
-                    qg_copy(i + ahead, r).start()
+                send_share(i + ahead)
 
             @pl.when(i == 1)
             def _():

time: 60.8 us -> 62.2 us (1.023)
  Pallas kernels: 59.4 us -> 60.7 us
    pallas_call x1, Pallas kernels: 57.9 us -> 59.3 us  [body(): pl.pallas_call(functools.partial(kernel, n_dp, n_cp, kv, grp, d, tok, pai...]
where the time goes in v5:
time: 62.2 us; the launch traced here: 62 us
  Pallas kernels  60.7 us (98%)
  between operations  1.29 us (2%)
    pallas_call x1, Pallas kernels, body(): pl.pallas_call(functools.partial(kernel, n_dp, n_cp, kv, grp, d, tok, pai...  59.3 us
    pallas_call x1, Pallas kernels, body(): pl.pallas_call(hand_out, out_shape=[jax.ShapeDtypeStruct(x.shape, x.dtype...  1.45 us

profile of v5, /device:TPU:0, one launch (start us, length us, event | category | flops | bytes accessed | tf_op | source)
XLA Modules:
  0.0 62.0 jit_solution(1786336127560855144)
XLA Ops:
  1.3 59.3 %shard_map.136 = (bf16[128,4096]{1,0:T(8,128)(2,1)S(1)}, bf16[128,4096]{1,0:T(8,128)(2,1)S(1)}, bf16[128,512]{1,0:T(8,128)(2,1)S(1)}, bf16[128,512]{1,0:T(8,128)(2,1)S(1)}, f32[8,128]{1,0:T(8,128)S(1)}) custom-call(bf16[128,4096]{1,0:T(8,128)(2,1)} %q_hbm.1, bf16[128,512]{1,0:T(8,128)(2,1)} %k_hbm.1, bf16[128,512]{1,0:T(8,128)(2,1)} %v_hbm.1, ...), custom_call_target="tpu_custom_call" | custom-call | tf_op jit(solution)/shard_map/pallas_call | solution.py:624
  60.6 1.4 %shard_map.137 = (bf16[128,4096]{1,0:T(8,128)(2,1)}, bf16[128,4096]{1,0:T(8,128)(2,1)}, bf16[128,512]{1,0:T(8,128)(2,1)}, bf16[128,512]{1,0:T(8,128)(2,1)}, f32[1,128]{1,0:T(1,128)}, /*index=5*/f32[1,128]{1,0:T(1,128)}) custom-call(bf16[128,4096]{1,0:T(8,128)(2,1)S(1)} %get-tuple-element.17.out, bf16[128,4096]{1,0:T(8,128)(2,1)S(1)} %get-tuple-element.18.dq, ...), custom_call_target="tpu_custom_call" | custom-call | tf_op jit(solution)/shard_map/pallas_call | solution.py:704

commit v6 on v4

--- a/solution.py
+++ b/solution.py
@@ -253,53 +253,61 @@
         ring_arrived(h, 4)
         start_if(ring_plan(h)[5])
 
-    def mate_copy(h, i):
+    halves = (slice(0, d), slice(d, 2 * d))
+
+    def mate_copy(h, i, p):
         return pltpu.make_async_remote_copy(
-            src_ref=grad_send.at[h, 2 * i],
-            dst_ref=gy_recv.at[h, i],
-            send_sem=gys_sem.at[h, i],
-            recv_sem=gyr_sem.at[h, i],
+            src_ref=grad_send.at[h, 2 * i, :, pl.ds(p * d, d)],
+            dst_ref=gy_recv.at[h, i, :, pl.ds(p * d, d)],
+            send_sem=gys_sem.at[h, i, p],
+            recv_sem=gyr_sem.at[h, i, p],
             device_id={"cp": mate},
             device_id_type=MESH,
         )
 
-    def front_copy(h, i):
+    def front_copy(h, i, p):
         return pltpu.make_async_remote_copy(
-            src_ref=grad_send.at[h, 3 - 2 * i],
-            dst_ref=gz_recv.at[h, i],
-            send_sem=gzs_sem.at[h, i],
-            recv_sem=gzr_sem.at[h, i],
+            src_ref=grad_send.at[h, 3 - 2 * i, :, pl.ds(p * d, d)],
+            dst_ref=gz_recv.at[h, i, :, pl.ds(p * d, d)],
+            send_sem=gzs_sem.at[h, i, p],
+            recv_sem=gzr_sem.at[h, i, p],
             device_id={"cp": front},
             device_id_type=MESH,
         )
 
     def after_mate(h):
-        for i in range(2):
-
-            @pl.when(mate >= 1 + 2 * i)
+        for p, at in enumerate(halves):
+            for i in range(2):
+
+                @pl.when(mate >= 1 + 2 * i)
+                def _():
+                    mate_copy(h, i, p).wait_recv()
+
+            one = gy_recv[h, 0, :, at].astype(F32)
+            three = gy_recv[h, 1, :, at].astype(F32)
+            last = sums[h, 2, :, at] + three * (1.0 - even_f)
+            grad_send[h, 3, :, at] = last.astype(BF16)
+
+            @pl.when(c >= 4)
             def _():
-                mate_copy(h, i).wait_recv()
-
-        one = gy_recv[h, 0].astype(F32)
-        three = gy_recv[h, 1].astype(F32)
-        sums[h, 0] = sums[h, 0] + one * even_f
-        sums[h, 1] = sums[h, 1] + three * even_f + one * (1.0 - even_f)
-        grad_send[h, 3] = (sums[h, 2] + three * (1.0 - even_f)).astype(BF16)
-
-        @pl.when(c >= 4)
-        def _():
-            front_copy(h, 0).start()
+                front_copy(h, 0, p).start()
+
+            sums[h, 0, :, at] = sums[h, 0, :, at] + one * even_f
+            sums[h, 1, :, at] = sums[h, 1, :, at] + three * even_f + one * (1.0 - even_f)
 
     def after_four(h):
-        @pl.when((c + 2 < n_cp) & (c >= 2))
-        def _():
-            front_copy(h, 0).wait_recv()
-
-        grad_send[h, 1] = (sums[h, 1] + gz_recv[h, 0].astype(F32)).astype(BF16)
-
-        @pl.when(c >= 2)
-        def _():
-            front_copy(h, 1).start()
+        for p, at in enumerate(halves):
+
+            @pl.when((c + 2 < n_cp) & (c >= 2))
+            def _():
+                front_copy(h, 0, p).wait_recv()
+
+            both = sums[h, 1, :, at] + gz_recv[h, 0, :, at].astype(F32)
+            grad_send[h, 1, :, at] = both.astype(BF16)
+
+            @pl.when(c >= 2)
+            def _():
+                front_copy(h, 1, p).start()
 
     for r in range(1, n_dp):
         kv_copy(r).start()
@@ -440,14 +448,15 @@
             if s % 2 == 1:
                 grad_send[h, s - 1, :, :d] = (dk_own[at, :] * inv_root).astype(BF16)
                 grad_send[h, s - 1, :, d:] = dv_own[at, :].astype(BF16)
-
-                @pl.when(c >= s)
-                def _():
-                    mate_copy(h, s // 2).start()
-
             else:
                 sums[h, s // 2, :, :d] = dk_own[at, :] * inv_root
                 sums[h, s // 2, :, d:] = dv_own[at, :]
+        for p in range(2):
+            for i in range(2):
+
+                @pl.when(c >= 1 + 2 * i)
+                def _():
+                    mate_copy(h, i, p).start()
 
         @pl.when(h == 0)
         def _():
@@ -488,7 +497,8 @@
 
         @pl.when(c + 2 < n_cp)
         def _():
-            front_copy(h, 1).wait_recv()
+            for p in range(2):
+                front_copy(h, 1, p).wait_recv()
 
         both = sums[h, 0] + gz_recv[h, 1].astype(F32)
         dk, dv = both[:, :d], both[:, d:]
@@ -570,11 +580,13 @@
 
             @pl.when(c >= 1 + 2 * i)
             def _():
-                mate_copy(h, i).wait_send()
+                for p in range(2):
+                    mate_copy(h, i, p).wait_send()
 
             @pl.when(c >= 4 - 2 * i)
             def _():
-                front_copy(h, i).wait_send()
+                for p in range(2):
+                    front_copy(h, i, p).wait_send()
 
         return carry
 
@@ -679,10 +691,10 @@
             dma((reach,)),
             dma((kv, 4)),
             dma((kv, reach)),
-            dma((kv, 2)),
-            dma((kv, 2)),
-            dma((kv, 2)),
-            dma((kv, 2)),
+            dma((kv, 2, 2)),
+            dma((kv, 2, 2)),
+            dma((kv, 2, 2)),
+            dma((kv, 2, 2)),
             dma((n_dp - 1,)),
             dma((n_dp - 1,)),
             dma((n_cp - 1,)),

time: 60.8 us -> 60.8 us (level)
  no operation moved by 1% of the time
where the time goes in v6:
time: 60.8 us; the launch traced here: 60.7 us
  Pallas kernels  59.4 us (98%)
  between operations  1.29 us (2%)
    pallas_call x1, Pallas kernels, body(): pl.pallas_call(functools.partial(kernel, n_dp, n_cp, kv, grp, d, tok, pai...  57.9 us
    pallas_call x1, Pallas kernels, body(): pl.pallas_call(hand_out, out_shape=[jax.ShapeDtypeStruct(x.shape, x.dtype...  1.45 us

profile of v6, /device:TPU:0, one launch (start us, length us, event | category | flops | bytes accessed | tf_op | source)
XLA Modules:
  0.0 60.7 jit_solution(12323426543863809971)
XLA Ops:
  1.3 57.9 %shard_map.136 = (bf16[128,4096]{1,0:T(8,128)(2,1)S(1)}, bf16[128,4096]{1,0:T(8,128)(2,1)S(1)}, bf16[128,512]{1,0:T(8,128)(2,1)S(1)}, bf16[128,512]{1,0:T(8,128)(2,1)S(1)}, f32[8,128]{1,0:T(8,128)S(1)}) custom-call(bf16[128,4096]{1,0:T(8,128)(2,1)} %q_hbm.1, bf16[128,512]{1,0:T(8,128)(2,1)} %k_hbm.1, bf16[128,512]{1,0:T(8,128)(2,1)} %v_hbm.1, ...), custom_call_target="tpu_custom_call" | custom-call | tf_op jit(solution)/shard_map/pallas_call | solution.py:630
  59.2 1.4 %shard_map.137 = (bf16[128,4096]{1,0:T(8,128)(2,1)}, bf16[128,4096]{1,0:T(8,128)(2,1)}, bf16[128,512]{1,0:T(8,128)(2,1)}, bf16[128,512]{1,0:T(8,128)(2,1)}, f32[1,128]{1,0:T(1,128)}, /*index=5*/f32[1,128]{1,0:T(1,128)}) custom-call(bf16[128,4096]{1,0:T(8,128)(2,1)S(1)} %get-tuple-element.17.out, bf16[128,4096]{1,0:T(8,128)(2,1)S(1)} %get-tuple-element.18.dq, ...), custom_call_target="tpu_custom_call" | custom-call | tf_op jit(solution)/shard_map/pallas_call | solution.py:710
